TPU v7x, 512 devices: a whole 4x4x16 slice. The times are simulated.
512 devices in a mesh: dp: 64 (over z, x_hi, core), rep: 8 (over y, x_lo).
Axes of the slice: x: 4 (x_hi: 2, x_lo: 2; x = x_hi * 2 + x_lo), y: 4, z: 16, core: 2. Of those that a mesh axis runs over, the one named last changes fastest.
Arguments:
- grad_out: bfloat16 [49152, 2048], P('dp', 'rep'), may hold values from -16 to 16
- pre_act: bfloat16 [49152, 3072], P('dp', 'rep'), may hold values from -6 to 6
- up_weight: bfloat16 [3072, 2048], P('rep'), may hold values from -0.125 to 0.125
- down_weight: bfloat16 [2048, 3072], P(None, 'rep'), may hold values from -0.109375 to 0.109375
- slot_counts: int32 [64], P('dp'), may hold values from 384 to 768, as said below
Outputs:
- input_grad: bfloat16 [49152, 2048], P('dp')
- down_grad: float32 [2048, 3072], P('dp', 'rep')
Inputs may be any that keep to these rules, and one draw needn't show every extreme that they name: Row i * 768 + j is live exactly when j < slot_counts[i]; some index has all 768 slots live and some index exactly 384.
All inputs are finite; a program needn't handle non-finite values.
Results may differ from a plain program's by a relative error of at most 0.0049.
Values may be sent and summed in bfloat16 or wider, within the bound.
No kernel may reach another device: no remote copies, remote signals or barrier semaphores. Data moves between devices by JAX's collectives and lax.ppermute only.
A program may use at most 64 MiB of HBM per device.

v0:
```python
import jax
import jax.numpy as jnp
from jax import lax
from jax.sharding import Mesh
from jax.sharding import PartitionSpec as P

REP = ("rep_0", "rep_1")


def whole_of(array, axes, dim):
    if not axes:
        return array
    nearer = lax.all_gather(array, axes[-1], axis=dim, tiled=True)
    return whole_of(nearer, axes[:-1], dim)


def on_device(grad_out, pre_act, up_weight, down_weight, slot_counts):
    slot_rows = grad_out.shape[0]
    live_rows = (lax.iota(jnp.int32, slot_rows) < slot_counts[0])[:, None]
    grad_full = whole_of(grad_out, REP, 1)
    grad_live = jnp.where(live_rows, grad_full, jnp.zeros_like(grad_full))
    zero_pre = jnp.zeros_like(pre_act)
    hidden = jnp.where(live_rows, jnp.maximum(pre_act, zero_pre), zero_pre)
    data_ranks = lax.axis_size("dp")
    down_sum = lax.psum_scatter(
        lax.dot_general(
            grad_live, hidden, (((0,), (0,)), ((), ())), preferred_element_type=jnp.float32
        ),
        "dp",
        scatter_dimension=0,
        tiled=True,
    )
    down_grad = down_sum / data_ranks
    hidden_grad = jnp.dot(grad_live, down_weight, preferred_element_type=jnp.float32)
    pre_grad = jnp.where(pre_act > 0, hidden_grad, jnp.zeros_like(hidden_grad)).astype(jnp.bfloat16)
    partial_terms = jnp.dot(pre_grad, up_weight, preferred_element_type=jnp.float32)
    input_sum = lax.psum(partial_terms, REP)
    input_grad = input_sum.astype(jnp.bfloat16)
    return (input_grad, down_grad)


def solution(mesh):
    finer = Mesh(mesh.devices.reshape(mesh.shape["dp"], 4, 2), ("dp", "rep_0", "rep_1"))
    in_specs = (P("dp", REP), P("dp", REP), P(REP, None), P(None, REP), P("dp"))
    out_specs = (P("dp", None), P("dp", REP))
    return jax.shard_map(
        on_device, mesh=finer, in_specs=in_specs, out_specs=out_specs, check_vma=False
    )
```

profile of v0, /device:TPU:4, one launch (start us, length us, event | category | flops | bytes accessed | tf_op | source)
XLA Modules:
  0.0 350.7 jit_solution(8490427789314710554)
XLA Ops:
  7.2 0.0 copy-start
  7.2 0.0 all-gather.2.cloned.1.call-start
  7.2 13.1 %all_gather.6 = bf16[768,512]{1,0:T(8,128)(2,1)} all-gather(bf16[768,256]{1,0:T(8,128)(2,1)} %param.5), channel_id=1, replica_groups=mesh['dp'=64,'rep_0'=4,'rep_1'=2] {'rep_1'}, dimensions={1}, use_global_device_ids=true | all-gather | bytes 1179648 | tf_op jit(solution)/shard_map/all_gather | solution.py:13
  20.3 0.0 all-gather.2.cloned.1.call-update
  20.4 0.0 reduce-scatter.2.cloned.1.call-start
  21.1 51.1 %all-gather.2.cloned.1.call-done = bf16[768,2048]{1,0:T(8,128)(2,1)} async-done(((bf16[768,512]{1,0:T(8,128)(2,1)}), bf16[768,2048]{1,0:T(8,128)(2,1)}) %all-gather.2.cloned.1.call-update) | async-done | bytes 3145744 | tf_op jit(solution)/shard_map/all_gather | solution.py:13
  72.2 5.6 %fusion.1 = f32[2048,384]{1,0:T(8,128)} fusion(bf16[768,2048]{1,0:T(8,128)(2,1)} %all-gather.2.cloned.1.call-done, pred[768]{0:T(1024)(128)(4,1)S(1)} %iota_compare_fusion, bf16[768,384]{1,0:T(8,128)(2,1)} %param.6), kind=kOutput, calls=%fused_computation.3 | convolution fusion | flops 1210122240 | bytes 6882048 | tf_op jit(solution)/shard_map/dot_general | solution.py:26
  77.8 0.0 copy-start.1
  77.8 0.0 reduce-scatter.2.cloned.1.call-update
  77.9 0.0 copy-done
  77.9 1.4 copy-done.1
  79.2 8.1 %fusion.2 = f32[768,2048]{1,0:T(8,128)} fusion(bf16[384,2048]{1,0:T(8,128)(2,1)S(1)} %copy-done, bf16[2048,384]{1,0:T(8,128)(2,1)S(1)} %copy-done.1, bf16[768,2048]{1,0:T(8,128)(2,1)} %all-gather.2.cloned.1.call-done, pred[768]{0:T(1024)(128)(4,1)S(1)} %iota_compare_fusion, bf16[768,384]{1,0:T(8,128)(2,1)} %param.6), kind=kOutput, calls=%fused_computation.4 | convolution fusion | flops 2418376704 | bytes 13173504 | tf_op jit(solution)/shard_map/dot_general | solution.py:36
  87.4 255.0 %all-reduce.1 = bf16[768,2048]{1,0:T(8,128)(2,1)} all-reduce(f32[768,2048]{1,0:T(8,128)} %fusion.2), channel_id=1, replica_groups=mesh['dp'=64,'rep_0'=4,'rep_1'=2] {'rep_0','rep_1'}, use_global_device_ids=true, to_apply=%region_0.1 | all-reduce | flops 1572864 | bytes 9437184 | tf_op jit(solution)/shard_map/psum | solution.py:37
  342.4 0.0 reduce-scatter.2.cloned.1.call-done
  342.4 1.4 broadcast_multiply_fusion
  (1 shorter events, 0.0 us)
Async XLA Ops:
  7.2 70.7 %copy-start = (bf16[384,2048]{1,0:T(8,128)(2,1)S(1)}, bf16[384,2048]{1,0:T(8,128)(2,1)}, u32[]{:S(2)}) copy-start(bf16[384,2048]{1,0:T(8,128)(2,1)} %param.7) | copy-start | bytes 4718596
  7.2 65.0 %all-gather.2.cloned.1.call-start = ((), (), s32[]{:S(2)}) async-start(), calls=%async_computation.1 | async-start | bytes 3932160 | tf_op jit(solution)/shard_map/all_gather | solution.py:13
  20.4 322.0 %reduce-scatter.2.cloned.1.call-start = ((), (), s32[]{:S(2)}) async-start(), calls=%async_computation.2 | async-start | bytes 3194880 | tf_op jit(solution)/shard_map/reduce_scatter | solution.py:25
  77.8 1.4 copy-start.1
Sparse Core Ops, SparseCore 0:
  20.5 51.6 all-gather.1
  78.0 225.9 reduce-scatter.1
where the time goes:
time: 351 us
  blocking collectives  268 us (76%)
  waiting for transfers between devices  51.2 us (15%)
  between operations  14.7 us (4%)
  matrix products  13.7 us (4%)
    psum x1, blocking collectives, on_device(): input_sum = lax.psum(partial_terms, REP)  255 us
    all_gather x1, waiting for transfers between devices, whole_of(): nearer = lax.all_gather(array, axes[-1], axis=dim, tiled=True)  51.1 us
    all_gather x1, blocking collectives, whole_of(): nearer = lax.all_gather(array, axes[-1], axis=dim, tiled=True)  13.1 us
    dot_general x1, matrix products, on_device(): jnp.dot(pre_grad, up_weight, preferred_element_type=jnp.float32)  8.12 us
  transfers between devices with their start and end apart: 2, of which 1 were waited for; matrix products, arithmetic and copies ran while one was open for 2% of the time, Pallas kernels for 0%

commit v1 on v0

--- a/solution.py
+++ b/solution.py
@@ -34,7 +34,7 @@
     hidden_grad = jnp.dot(grad_live, down_weight, preferred_element_type=jnp.float32)
     pre_grad = jnp.where(pre_act > 0, hidden_grad, jnp.zeros_like(hidden_grad)).astype(jnp.bfloat16)
     partial_terms = jnp.dot(pre_grad, up_weight, preferred_element_type=jnp.float32)
-    input_sum = lax.psum(partial_terms, REP)
+    input_sum = jnp.sum(lax.all_gather(partial_terms, REP), axis=0)
     input_grad = input_sum.astype(jnp.bfloat16)
     return (input_grad, down_grad)
 

time: 351 us -> 1290 us (3.68)
  the two profiles are of different devices: /device:TPU:4 before, /device:TPU:1 now
where the time goes in v1:
time: 1290 us
  waiting for transfers between devices  1220 us (95%)
  other arithmetic  21.1 us (2%)
  between operations  14.4 us (1%)
  matrix products  13.7 us (1%)
    all_gather x1, waiting for transfers between devices, on_device(): input_sum = jnp.sum(lax.all_gather(partial_terms, REP), axis=0)  971 us
    reduce_scatter x1, waiting for transfers between devices, on_device(): lax.psum_scatter(lax.dot_general(grad_live, hidden, (((0,), (0,)), ((), (...  198 us
    all_gather x1, waiting for transfers between devices, whole_of(): nearer = lax.all_gather(array, axes[-1], axis=dim, tiled=True)  55.1 us
  transfers between devices with their start and end apart: 3, of which 3 were waited for; matrix products, arithmetic and copies ran while one was open for 1% of the time, Pallas kernels for 0%

profile of v1, /device:TPU:1, one launch (start us, length us, event | category | flops | bytes accessed | tf_op | source)
XLA Modules:
  0.0 1285.2 jit_solution(15383877522979706606)
XLA Ops:
  7.2 0.0 copy-start
  7.2 0.0 all-gather.4.cloned.1.call-start
  7.2 10.0 all_gather.12
  17.3 0.0 all-gather.4.cloned.1.call-update
  17.3 0.0 reduce-scatter.2.cloned.1.call-start
  18.0 55.1 %all-gather.4.cloned.1.call-done = bf16[768,2048]{1,0:T(8,128)(2,1)} async-done(((bf16[768,512]{1,0:T(8,128)(2,1)}), bf16[768,2048]{1,0:T(8,128)(2,1)}) %all-gather.4.cloned.1.call-update) | async-done | bytes 3145744 | tf_op jit(solution)/shard_map/all_gather | solution.py:13
  73.1 5.7 fusion.1
  78.7 0.0 copy-start.2
  78.7 0.0 reduce-scatter.2.cloned.1.call-update
  78.7 0.0 all-gather.6.cloned.1.call-start
  78.8 0.0 copy-done
  78.8 1.3 copy-done.2
  80.1 8.1 fusion.2
  88.2 0.0 all-gather.6.cloned.1.call-update
  88.2 198.0 %reduce-scatter.2.cloned.1.call-done = f32[32,384]{1,0:T(8,128)} async-done(((f32[2048,384]{1,0:T(8,128)}), f32[32,384]{1,0:T(8,128)}) %reduce-scatter.2.cloned.1.call-update) | async-done | bytes 49168 | tf_op jit(solution)/shard_map/reduce_scatter | solution.py:25
  286.2 1.4 broadcast_multiply_fusion
  287.6 971.4 %all-gather.6.cloned.1.call-done = f32[6144,2048]{1,0:T(8,128)} async-done(((f32[768,2048]{1,0:T(8,128)}), f32[6144,2048]{1,0:T(8,128)}) %all-gather.6.cloned.1.call-update) | async-done | bytes 50331664 | tf_op jit(solution)/shard_map/all_gather | solution.py:37
  1259.0 0.0 copy-start.1
  1259.0 19.7 %reduce_sum.9 = bf16[768,2048]{1,0:T(8,128)(2,1)} reduce(f32[8,768,2048]{2,1,0:T(8,128)} %bitcast.5, f32[]{:T(128)} %constant.4.clone.1), dimensions={0}, to_apply=%region_0.1 | reduce | flops 11010048 | bytes 53477380 | tf_op jit(solution)/shard_map/reduce_sum | solution.py:37
  1278.7 0.0 copy-done.1
  (1 shorter events, 0.0 us)
Async XLA Ops:
  7.2 71.6 %copy-start = (bf16[384,2048]{1,0:T(8,128)(2,1)S(1)}, bf16[384,2048]{1,0:T(8,128)(2,1)}, u32[]{:S(2)}) copy-start(bf16[384,2048]{1,0:T(8,128)(2,1)} %param.7) | copy-start | bytes 4718596
  7.2 65.9 %all-gather.4.cloned.1.call-start = ((), (), s32[]{:S(2)}) async-start(), calls=%async_computation.1 | async-start | bytes 3932160 | tf_op jit(solution)/shard_map/all_gather | solution.py:13
  17.3 268.9 %reduce-scatter.2.cloned.1.call-start = ((), (), s32[]{:S(2)}) async-start(), calls=%async_computation.2 | async-start | bytes 3194880 | tf_op jit(solution)/shard_map/reduce_scatter | solution.py:25
  78.7 1.4 copy-start.2
  78.7 1180.3 %all-gather.6.cloned.1.call-start = ((), (), s32[]{:S(2)}) async-start(), calls=%async_computation.3 | async-start | bytes 56623104 | tf_op jit(solution)/shard_map/all_gather | solution.py:37
  1259.0 19.7 %copy-start.1 = (bf16[384,2048]{1,0:T(8,128)(2,1)S(1)}, bf16[384,2048]{1,0:T(8,128)(2,1)}, u32[]{:S(2)}) copy-start(bf16[384,2048]{1,0:T(8,128)(2,1)} %param.7) | copy-start | bytes 4718596
Sparse Core Ops, SparseCore 0:
  17.4 55.6 all-gather.3
  78.9 207.2 reduce-scatter.1
  288.3 970.7 all-gather.5

commit v2 on v0

--- a/solution.py
+++ b/solution.py
@@ -34,7 +34,7 @@
     hidden_grad = jnp.dot(grad_live, down_weight, preferred_element_type=jnp.float32)
     pre_grad = jnp.where(pre_act > 0, hidden_grad, jnp.zeros_like(hidden_grad)).astype(jnp.bfloat16)
     partial_terms = jnp.dot(pre_grad, up_weight, preferred_element_type=jnp.float32)
-    input_sum = lax.psum(partial_terms, REP)
+    input_sum = lax.psum(lax.psum(partial_terms, "rep_1"), "rep_0")
     input_grad = input_sum.astype(jnp.bfloat16)
     return (input_grad, down_grad)
 

time: 351 us -> 592 us (1.69)
  waiting for transfers between devices: 51.2 us -> 434 us
  blocking collectives: 268 us -> 127 us
    reduce_scatter x1, waiting for transfers between devices: 0.01 us -> 208 us  [on_device(): lax.psum_scatter(lax.dot_general(grad_live, hidden, (((0,), (0,)), ((), (...]
    psum x0 -> x1, waiting for transfers between devices: none -> 175 us  [on_device(): input_sum = lax.psum(lax.psum(partial_terms, 'rep_1'), 'rep_0')]
    psum x1, blocking collectives: 255 us -> 114 us  [on_device(): input_sum = lax.psum(lax.psum(partial_terms, 'rep_1'), 'rep_0')]
  transfers between devices with their start and end apart: 2 -> 3, of which waited for: 1 -> 3; matrix products, arithmetic and copies ran while one was open for 2% -> 2% of each run, Pallas kernels for 0% -> 0%
where the time goes in v2:
time: 592 us
  waiting for transfers between devices  434 us (73%)
  blocking collectives  127 us (21%)
  between operations  14.4 us (2%)
  matrix products  13.8 us (2%)
    reduce_scatter x1, waiting for transfers between devices, on_device(): lax.psum_scatter(lax.dot_general(grad_live, hidden, (((0,), (0,)), ((), (...  208 us
    psum x1, waiting for transfers between devices, on_device(): input_sum = lax.psum(lax.psum(partial_terms, 'rep_1'), 'rep_0')  175 us
    psum x1, blocking collectives, on_device(): input_sum = lax.psum(lax.psum(partial_terms, 'rep_1'), 'rep_0')  114 us
    all_gather x1, waiting for transfers between devices, whole_of(): nearer = lax.all_gather(array, axes[-1], axis=dim, tiled=True)  51.1 us
    all_gather x1, blocking collectives, whole_of(): nearer = lax.all_gather(array, axes[-1], axis=dim, tiled=True)  13.1 us
  transfers between devices with their start and end apart: 3, of which 3 were waited for; matrix products, arithmetic and copies ran while one was open for 2% of the time, Pallas kernels for 0%

profile of v2, /device:TPU:4, one launch (start us, length us, event | category | flops | bytes accessed | tf_op | source)
XLA Modules:
  0.0 592.0 jit_solution(7643836721390185781)
XLA Ops:
  7.2 0.0 copy-start
  7.2 0.0 all-gather.2.cloned.1.call-start
  7.2 13.1 %all_gather.6 = bf16[768,512]{1,0:T(8,128)(2,1)} all-gather(bf16[768,256]{1,0:T(8,128)(2,1)} %param.5), channel_id=1, replica_groups=mesh['dp'=64,'rep_0'=4,'rep_1'=2] {'rep_1'}, dimensions={1}, use_global_device_ids=true | all-gather | bytes 1179648 | tf_op jit(solution)/shard_map/all_gather | solution.py:13
  20.3 0.0 all-gather.2.cloned.1.call-update
  20.4 0.0 reduce-scatter.2.cloned.1.call-start
  21.1 51.1 %all-gather.2.cloned.1.call-done = bf16[768,2048]{1,0:T(8,128)(2,1)} async-done(((bf16[768,512]{1,0:T(8,128)(2,1)}), bf16[768,2048]{1,0:T(8,128)(2,1)}) %all-gather.2.cloned.1.call-update) | async-done | bytes 3145744 | tf_op jit(solution)/shard_map/all_gather | solution.py:13
  72.2 5.7 fusion.1
  77.9 0.0 copy-start.1
  77.9 0.0 reduce-scatter.2.cloned.1.call-update
  77.9 0.0 all-reduce.3.cloned.1.call-start
  77.9 0.0 copy-done
  77.9 1.3 copy-done.1
  79.3 8.1 %fusion.2 = f32[768,2048]{1,0:T(8,128)} fusion(bf16[384,2048]{1,0:T(8,128)(2,1)S(1)} %copy-done, bf16[2048,384]{1,0:T(8,128)(2,1)S(1)} %copy-done.1, bf16[768,2048]{1,0:T(8,128)(2,1)} %all-gather.2.cloned.1.call-done, pred[768]{0:T(1024)(128)(4,1)S(1)} %iota_compare_fusion, bf16[768,384]{1,0:T(8,128)(2,1)} %param.6), kind=kOutput, calls=%fused_computation.4 | convolution fusion | flops 2418376704 | bytes 13173504 | tf_op jit(solution)/shard_map/dot_general | solution.py:36
  87.4 0.0 all-reduce.3.cloned.1.call-update
  87.4 208.0 %reduce-scatter.2.cloned.1.call-done = f32[32,384]{1,0:T(8,128)} async-done(((f32[2048,384]{1,0:T(8,128)}), f32[32,384]{1,0:T(8,128)}) %reduce-scatter.2.cloned.1.call-update) | async-done | bytes 49168 | tf_op jit(solution)/shard_map/reduce_scatter | solution.py:25
  295.4 1.4 broadcast_multiply_fusion
  296.8 174.7 %all-reduce.3.cloned.1.call-done = f32[768,2048]{1,0:T(8,128)} async-done(((f32[768,2048]{1,0:T(8,128)}), f32[768,2048]{1,0:T(8,128)}) %all-reduce.3.cloned.1.call-update) | async-done | bytes 6291472 | tf_op jit(solution)/shard_map/psum | solution.py:37
  471.5 113.9 %all-reduce.4 = bf16[768,2048]{1,0:T(8,128)(2,1)} all-reduce(f32[768,2048]{1,0:T(8,128)} %all-reduce.3.cloned.1.call-done), channel_id=1, replica_groups=mesh['dp'=64,'rep_0'=4,'rep_1'=2] {'rep_0'}, use_global_device_ids=true, to_apply=%region_1.2 | all-reduce | flops 1572864 | bytes 9437184 | tf_op jit(solution)/shard_map/psum | solution.py:37
  (1 shorter events, 0.0 us)
Async XLA Ops:
  7.2 70.8 %copy-start = (bf16[384,2048]{1,0:T(8,128)(2,1)S(1)}, bf16[384,2048]{1,0:T(8,128)(2,1)}, u32[]{:S(2)}) copy-start(bf16[384,2048]{1,0:T(8,128)(2,1)} %param.7) | copy-start | bytes 4718596
  7.2 65.0 %all-gather.2.cloned.1.call-start = ((), (), s32[]{:S(2)}) async-start(), calls=%async_computation.1 | async-start | bytes 3932160 | tf_op jit(solution)/shard_map/all_gather | solution.py:13
  20.4 275.0 %reduce-scatter.2.cloned.1.call-start = ((), (), s32[]{:S(2)}) async-start(), calls=%async_computation.3 | async-start | bytes 3194880 | tf_op jit(solution)/shard_map/reduce_scatter | solution.py:25
  77.9 1.4 copy-start.1
  77.9 393.6 %all-reduce.3.cloned.1.call-start = ((), (), s32[]{:S(2)}) async-start(), calls=%async_computation.2 | async-start | bytes 12582912 | tf_op jit(solution)/shard_map/psum | solution.py:37
Sparse Core Ops, SparseCore 0:
  20.5 51.6 all-gather.1
  78.0 217.3 reduce-scatter.1
  298.4 173.0 all-reduce.2
